TPU v7x, 32 devices: a whole 2x2x4 slice. The times are simulated.
32 devices in a mesh: col: 4 (over x, core), gx: 4 (over z), gy: 2 (over y).
Axes of the slice: x: 2, y: 2, z: 4, core: 2. Of those that a mesh axis runs over, the one named last changes fastest.
Arguments:
- volume: float32 [32, 8, 16, 256], P('col', None, 'gx', 'gy'), may hold values from -6 to 6
- filters: float32 [32, 32, 3, 3, 3], P('col'), may hold values from -0.21875 to 0.21875
- upstream: float32 [32, 8, 16, 256], P('col', None, 'gx', 'gy'), may hold values from -6 to 6
Outputs:
- response: float32 [32, 8, 16, 256], P('col', None, 'gx', 'gy')
- input_grad: float32 [32, 8, 16, 256], P('col', None, 'gx', 'gy')
- filter_grad: float32 [32, 32, 3, 3, 3], P('col')
All inputs are finite; a program needn't handle non-finite values.
Results may differ from a plain program's by a relative error of at most 0.0003.
Values sent between devices are 32-bit elements; how exact they have to be, the bound alone decides.
A program may use at most 64 MiB of HBM per device.

v0:
```python
import functools

import jax
import jax.numpy as jnp
from jax import lax
from jax.experimental import pallas as pl
from jax.experimental.pallas import tpu as pltpu
from jax.sharding import PartitionSpec as P

MESH = pl.DeviceIdType.MESH
F32 = jnp.float32
BF16 = jnp.bfloat16
DIRS = [(-1, 0), (1, 0), (-1, -1), (0, -1), (1, -1), (-1, 1), (0, 1), (1, 1)]
TAPS = [(a, b, e) for a in range(3) for b in range(3) for e in range(3)]
PIECES = 7


def split(value):
    high = value.astype(BF16).astype(F32)
    return jnp.concatenate([high, value - high], axis=0).astype(BF16)


def kernel(
    nx, ny, planes, rows, scale,
    v_hbm, w_hbm, u_hbm,
    resp_ref, grad_ref, fg_ref,
    v_in, w_in, u_in, vx, x2, u_own, u_row, pack_out, pack_in, u3, igp, rs,
    acc, local, row_in, rpack_out, rpack_in, gpack, grecv, gfin,
    in_sem, v_send, v_recv, u_send, u_recv, g_send, g_recv, r_send, r_recv,
    s1_send, s1_recv, s2_send, s2_recv,
):
    col, gx, gy = lax.axis_index("col"), lax.axis_index("gx"), lax.axis_index("gy")
    group = nx * ny
    me = gx * ny + gy
    cells = planes * rows
    low, high = col % 2, col // 2
    core = high * 2 + (1 - low)
    chip = (1 - high) * 2 + low
    far = (1 - high) * 2 + (1 - low)

    def exists(dx, dy):
        ok = None
        for d, at, size in ((dx, gx, nx), (dy, gy, ny)):
            if d:
                term = (at + d >= 0) & (at + d < size)
                ok = term if ok is None else ok & term
        return ok

    loads = [
        pltpu.make_async_copy(s, d, in_sem.at[i])
        for i, (s, d) in enumerate(((v_hbm, v_in), (u_hbm, u_in), (w_hbm, w_in)))
    ]
    for load in loads:
        load.start()
    barrier = pltpu.get_barrier_semaphore()

    u_row[...] = jnp.zeros_like(u_row)
    pack_in[...] = jnp.zeros_like(pack_in)
    row_in[...] = jnp.zeros_like(row_in)
    rpack_in[...] = jnp.zeros_like(rpack_in)

    for other in (core, chip):
        pl.semaphore_signal(barrier, inc=1, device_id={"col": other}, device_id_type=MESH)

    def greet(j, carry):
        @pl.when(j != me)
        def _():
            pl.semaphore_signal(
                barrier, inc=1, device_id={"gx": j // ny, "gy": j % ny}, device_id_type=MESH
            )
        return carry

    lax.fori_loop(0, group, greet, 0)

    lane = lax.broadcasted_iota(jnp.int32, (8, 128), 1)
    loads[0].wait()
    for i in range(cells):
        vx[col, i] = v_in[pl.ds(i, 8, stride=cells), :]
    loads[1].wait()
    for i in range(cells):
        u_own[i // rows, i % rows] = u_in[pl.ds(i, 8, stride=cells), :]
    pack = jnp.zeros((8, 128), F32)
    for z in range(planes):
        for x in range(rows):
            at = z * 8 + x + 1
            tile = u_own[z, x]
            pack = jnp.where(lane == at, pltpu.roll(tile, at + 1, 1), pack)
            pack = jnp.where(lane == at + 64, pltpu.roll(tile, at + 64, 1), pack)
    pack_out[...] = pack

    pl.semaphore_wait(barrier, group + 1)

    def v_copy(slot, sem, target):
        return pltpu.make_async_remote_copy(
            src_ref=vx.at[slot], dst_ref=vx.at[slot], send_sem=v_send.at[sem],
            recv_sem=v_recv.at[sem], device_id={"col": target}, device_id_type=MESH,
        )

    def u_copy(d):
        dx, dy = DIRS[d]
        if dy == 0:
            src = u_own.at[:, 0 if dx < 0 else rows - 1]
            dst = u_row.at[d]
        else:
            src, dst = pack_out, pack_in.at[d - 2]
        return pltpu.make_async_remote_copy(
            src_ref=src, dst_ref=dst, send_sem=u_send.at[d], recv_sem=u_recv.at[d],
            device_id={"gx": gx + dx, "gy": gy + dy}, device_id_type=MESH,
        )

    def r_copy(d):
        dx, dy = DIRS[d]
        if dy == 0:
            src, dst = local.at[0 if dx < 0 else rows + 1], row_in.at[d]
        else:
            src, dst = rpack_out, rpack_in.at[d - 2]
        return pltpu.make_async_remote_copy(
            src_ref=src, dst_ref=dst, send_sem=r_send.at[d], recv_sem=r_recv.at[d],
            device_id={"gx": gx + dx, "gy": gy + dy}, device_id_type=MESH,
        )

    def each(copies, what, sender):
        for d, (dx, dy) in enumerate(DIRS):
            @pl.when(exists(dx, dy) if sender else exists(-dx, -dy))
            def _():
                getattr(copies(d), what)()

    each(u_copy, "start", True)
    v_chip, v_core = v_copy(col, 0, chip), v_copy(col, 1, core)
    v_chip.start()
    v_core.start()

    loads[2].wait()
    w = w_in[...]
    taps8 = w.shape[0]
    w_hi = w.astype(BF16)
    w_lo = (w - w_hi.astype(F32)).astype(BF16)
    c_at = lax.broadcasted_iota(jnp.int32, (32, 128), 0)
    k_at = lax.broadcasted_iota(jnp.int32, (32, 128), 1)
    same = ((k_at % 64) // 16 == c_at // 8) & (k_at % 8 == c_at % 8)
    pick_hi = jnp.where(same & (k_at < 64), 1.0, 0.0).astype(BF16)
    pick_lo = jnp.where(same & (k_at >= 64), 1.0, 0.0).astype(BF16)
    w_fwd = (
        jnp.dot(w_hi, pick_hi, preferred_element_type=F32)
        + jnp.dot(w_lo, pick_lo, preferred_element_type=F32)
    ).astype(BF16)
    eye_r = lax.broadcasted_iota(jnp.int32, (32, 32), 0)
    eye_c = lax.broadcasted_iota(jnp.int32, (32, 32), 1)
    eye = jnp.where(eye_r == eye_c, 1.0, 0.0).astype(BF16)
    d_r = lax.broadcasted_iota(jnp.int32, (taps8, 2 * taps8), 0)
    d_c = lax.broadcasted_iota(jnp.int32, (taps8, 2 * taps8), 1)
    twice = jnp.where((d_r // 8 == d_c // 16) & (d_r % 8 == d_c % 8), 1.0, 0.0).astype(BF16)
    nt = (((1,), (1,)), ((), ()))
    w_back = []
    for part in (w_hi, w_lo):
        turned = lax.dot_general(eye, part, nt, preferred_element_type=F32).astype(BF16)
        w_back.append(jnp.dot(turned, twice, preferred_element_type=F32))
    w_back = jnp.concatenate(w_back, axis=0).astype(BF16)

    each(u_copy, "wait_recv", False)
    spot = lane % 8
    edge = jnp.zeros((8, 128), F32)
    for first, keep in ((3, lane < 64), (0, lane >= 64)):
        before, mid, after = pack_in[first + 2], pack_in[first + 1], pack_in[first]
        total = jnp.where((spot >= 1) & (spot <= rows), mid, 0.0)
        total = jnp.where(spot == 0, pltpu.roll(before, 128 - rows, 1), total)
        total = jnp.where(spot == rows + 1, pltpu.roll(after, rows, 1), total)
        edge = jnp.where(keep, total, edge)
    zero16 = jnp.zeros((16, 128), BF16)
    for e in range(3):
        for x in range(rows + 2):
            u3[e, 0, x] = zero16
            u3[e, planes + 1, x] = zero16
    for z in range(planes):
        for x in range(rows + 2):
            at = z * 8 + x
            if x == 0:
                tile = u_row[1, z]
            elif x == rows + 1:
                tile = u_row[0, z]
            else:
                tile = u_own[z, x - 1]
            left = jnp.where(
                lane == 127, pltpu.roll(edge, (127 - 64 - at) % 128, 1), pltpu.roll(tile, 127, 1)
            )
            right = jnp.where(
                lane == 0, pltpu.roll(edge, (128 - at) % 128, 1), pltpu.roll(tile, 1, 1)
            )
            u3[0, z + 1, x] = split(left)
            u3[1, z + 1, x] = split(tile)
            u3[2, z + 1, x] = split(right)

    def stack(z):
        return jnp.concatenate(
            [
                jnp.concatenate([u3[e, z + 2 - a, x + 2 - b] for a, b, e in TAPS], axis=0)
                for x in range(rows)
            ],
            axis=1,
        )

    def back(z, carry):
        both = jnp.dot(w_back, stack(z), preferred_element_type=F32)
        for g in range(4):
            for x in range(rows):
                lanes = slice(x * 128, (x + 1) * 128)
                igp[g, z * rows + x] = (
                    both[g * 8 : g * 8 + 8, lanes] + both[32 + g * 8 : 40 + g * 8, lanes]
                )
        return carry

    lax.fori_loop(0, planes, back, 0)

    def g_copy(slot, to, target):
        return pltpu.make_async_remote_copy(
            src_ref=igp.at[slot], dst_ref=rs.at[to], send_sem=g_send.at[to],
            recv_sem=g_recv.at[to], device_id={"col": target}, device_id_type=MESH,
        )

    g_far, g_core, g_chip = g_copy(far, 1, core), g_copy(core, 0, core), g_copy(chip, 2, chip)
    g_far.start()
    v_chip.wait_recv()
    v_fwd = v_copy(chip, 2, core)
    v_fwd.start()
    g_core.start()
    g_far.wait_recv()
    for i in range(cells):
        igp[chip, i] = igp[chip, i] + rs[1, i]
    g_chip.start()

    v_core.wait_recv()
    for g in (col, chip, core):
        for i in range(cells):
            x2[g, i] = split(vx[g, i])
    v_fwd.wait_recv()
    for i in range(cells):
        x2[far, i] = split(vx[far, i])

    def block(z):
        return jnp.concatenate(
            [
                jnp.concatenate([x2[g, z * rows + x] for g in range(4)], axis=0)
                for x in range(rows)
            ],
            axis=1,
        )

    def weigh(z, total):
        return total + lax.dot_general(block(z), stack(z), nt, preferred_element_type=F32)

    total = lax.fori_loop(0, planes, weigh, jnp.zeros((64, 2 * taps8), F32))
    folded = jnp.concatenate(
        [total[g * 16 : g * 16 + 8] + total[g * 16 + 8 : g * 16 + 16] for g in range(4)], axis=0
    )
    wide = jnp.concatenate(
        [folded, jnp.zeros((32, 512 - 2 * taps8), F32)], axis=1
    )
    wide = jnp.concatenate([wide, jnp.zeros((96, 512), F32)], axis=0)
    for p in range(PIECES):
        if p % 2 == 0:
            turned = wide[:, (p // 2) * 128 : (p // 2 + 1) * 128].T
        tile = jnp.zeros((8, 128), F32)
        for q in range(4):
            at = (p % 2) * 64 + q * 16
            term = turned[at : at + 8] + turned[at + 8 : at + 16]
            tile = tile + (pltpu.roll(term, q * 32, 1) if q else term)
        gpack[p] = tile

    def s1_copy(i):
        return pltpu.make_async_remote_copy(
            src_ref=gpack.at[i], dst_ref=grecv.at[me], send_sem=s1_send.at[i],
            recv_sem=s1_recv.at[me], device_id={"gx": i // ny, "gy": i % ny}, device_id_type=MESH,
        )

    for i in range(PIECES):
        @pl.when(me != i)
        def _():
            s1_copy(i).start()

    acc[...] = jnp.zeros_like(acc)

    def forward(z, carry):
        cell = block(z)
        y = jnp.dot(w_fwd, jnp.concatenate([cell, cell], axis=0), preferred_element_type=F32)
        for a in range(3):
            for e in range(3):
                for x in range(rows + 2):
                    terms = [
                        y[
                            ((a * 3 + b) * 3 + e) * 8 : ((a * 3 + b) * 3 + e) * 8 + 8,
                            (x + b - 2) * 128 : (x + b - 1) * 128,
                        ]
                        for b in range(3)
                        if 0 <= x + b - 2 < rows
                    ]
                    acc[e, z + 2 - a, x] = functools.reduce(lambda s, t: s + t, terms, acc[e, z + 2 - a, x])
        return carry

    lax.fori_loop(0, planes, forward, 0)
    pack = jnp.zeros((8, 128), F32)
    for z in range(planes):
        for x in range(rows + 2):
            at = z * 8 + x
            up, down = acc[0, z + 1, x], acc[2, z + 1, x]
            pack = jnp.where(lane == at, pltpu.roll(up, at + 1, 1), pack)
            pack = jnp.where(lane == at + 64, pltpu.roll(down, at + 64, 1), pack)
            local[x, z] = (
                acc[1, z + 1, x]
                + jnp.where(lane == 0, 0.0, pltpu.roll(up, 1, 1))
                + jnp.where(lane == 127, 0.0, pltpu.roll(down, 127, 1))
            )
    rpack_out[...] = pack
    each(r_copy, "start", True)

    def s2_copy(i, j):
        return pltpu.make_async_remote_copy(
            src_ref=gfin.at[i], dst_ref=gfin.at[i], send_sem=s2_send.at[j],
            recv_sem=s2_recv.at[i], device_id={"gx": j // ny, "gy": j % ny}, device_id_type=MESH,
        )

    def s1_arrival(j):
        return pltpu.make_async_remote_copy(
            src_ref=gpack.at[0], dst_ref=grecv.at[j], send_sem=s1_send.at[0],
            recv_sem=s1_recv.at[j], device_id={"gx": j // ny, "gy": j % ny}, device_id_type=MESH,
        )

    @pl.when(me < PIECES)
    def _():
        grecv[me] = gpack[me]

        def collect(j, total):
            @pl.when(j != me)
            def _():
                s1_arrival(j).wait_recv()
            return total + grecv[j]

        gfin[me] = lax.fori_loop(0, group, collect, jnp.zeros((8, 128), F32)) * scale

        def hand_out(j, carry):
            @pl.when(j != me)
            def _():
                s2_copy(me, j).start()
            return carry

        lax.fori_loop(0, group, hand_out, 0)

    g_core.wait_recv()
    g_chip.wait_recv()
    for i in range(cells):
        grad_ref[pl.ds(i, 8, stride=cells), :] = igp[col, i] + rs[0, i] + rs[2, i]

    each(r_copy, "wait_recv", False)
    edge = jnp.zeros((8, 128), F32)
    for first, keep in ((3, lane < 64), (0, lane >= 64)):
        before, mid, after = rpack_in[first + 2], rpack_in[first + 1], rpack_in[first]
        total = mid + jnp.where(spot == 1, pltpu.roll(before, 128 - rows, 1), 0.0)
        total = total + jnp.where(spot == rows, pltpu.roll(after, rows, 1), 0.0)
        edge = jnp.where(keep, total, edge)
    for z in range(planes):
        for x in range(rows):
            at = z * 8 + x + 1
            tile = local[x + 1, z]
            if x == 0:
                tile = tile + row_in[1, z]
            if x == rows - 1:
                tile = tile + row_in[0, z]
            tile = tile + jnp.where(lane == 0, pltpu.roll(edge, 128 - at, 1), 0.0)
            tile = tile + jnp.where(lane == 127, pltpu.roll(edge, (127 - 64 - at) % 128, 1), 0.0)
            resp_ref[pl.ds(z * rows + x, 8, stride=cells), :] = tile

    for i in range(PIECES):
        @pl.when(me != i)
        def _():
            s2_copy(i, i).wait_recv()
        for q in range(4):
            if i * 4 + q < 27:
                tile = gfin[i]
                if q:
                    tile = pltpu.roll(tile, 128 - q * 32, 1)
                fg_ref[(i * 4 + q) * 8 : (i * 4 + q) * 8 + 8, :] = tile[:, :32]

    each(u_copy, "wait_send", True)
    each(r_copy, "wait_send", True)
    for copy in (v_chip, v_core, v_fwd, g_far, g_core, g_chip):
        copy.wait_send()
    for i in range(PIECES):
        @pl.when(me != i)
        def _():
            s1_copy(i).wait_send()

    @pl.when(me < PIECES)
    def _():
        def left(j, carry):
            @pl.when(j != me)
            def _():
                s2_copy(me, j).wait_send()
            return carry

        lax.fori_loop(0, group, left, 0)


def solution(mesh):
    nx, ny = mesh.shape["gx"], mesh.shape["gy"]

    def shards(volume, filters, upstream):
        own, planes, rows, width = volume.shape
        cells = planes * rows
        scale = (planes * rows * nx * width * ny) ** (-0.5)
        weights = filters.transpose(2, 3, 4, 0, 1).reshape(27 * own, 32)
        tile = (8, 128)
        resp, grad, fg = pl.pallas_call(
            functools.partial(kernel, nx, ny, planes, rows, scale),
            out_shape=(
                jax.ShapeDtypeStruct((own * cells, width), F32),
                jax.ShapeDtypeStruct((own * cells, width), F32),
                jax.ShapeDtypeStruct((27 * own, 32), F32),
            ),
            in_specs=[pl.BlockSpec(memory_space=pl.ANY)] * 3,
            out_specs=(pl.BlockSpec(memory_space=pltpu.VMEM),) * 3,
            scratch_shapes=[
                pltpu.VMEM((own * cells, width), F32),
                pltpu.VMEM((27 * own, 32), F32),
                pltpu.VMEM((own * cells, width), F32),
                pltpu.VMEM((4, cells) + tile, F32),
                pltpu.VMEM((4, cells, 16, 128), BF16),
                pltpu.VMEM((planes, rows) + tile, F32),
                pltpu.VMEM((2, planes) + tile, F32),
                pltpu.VMEM(tile, F32),
                pltpu.VMEM((6,) + tile, F32),
                pltpu.VMEM((3, planes + 2, rows + 2, 16, 128), BF16),
                pltpu.VMEM((4, cells) + tile, F32),
                pltpu.VMEM((3, cells) + tile, F32),
                pltpu.VMEM((3, planes + 2, rows + 2) + tile, F32),
                pltpu.VMEM((rows + 2, planes) + tile, F32),
                pltpu.VMEM((2, planes) + tile, F32),
                pltpu.VMEM(tile, F32),
                pltpu.VMEM((6,) + tile, F32),
                pltpu.VMEM((PIECES,) + tile, F32),
                pltpu.VMEM((nx * ny,) + tile, F32),
                pltpu.VMEM((PIECES,) + tile, F32),
                pltpu.SemaphoreType.DMA((3,)),
                pltpu.SemaphoreType.DMA((3,)),
                pltpu.SemaphoreType.DMA((3,)),
                pltpu.SemaphoreType.DMA((8,)),
                pltpu.SemaphoreType.DMA((8,)),
                pltpu.SemaphoreType.DMA((3,)),
                pltpu.SemaphoreType.DMA((3,)),
                pltpu.SemaphoreType.DMA((8,)),
                pltpu.SemaphoreType.DMA((8,)),
                pltpu.SemaphoreType.DMA((PIECES,)),
                pltpu.SemaphoreType.DMA((nx * ny,)),
                pltpu.SemaphoreType.DMA((nx * ny,)),
                pltpu.SemaphoreType.DMA((PIECES,)),
            ],
            compiler_params=pltpu.CompilerParams(
                collective_id=0, has_side_effects=True, vmem_limit_bytes=40 * 1024 * 1024
            ),
        )(
            volume.reshape(own * cells, width),
            weights,
            upstream.reshape(own * cells, width),
        )
        return (
            resp.reshape(volume.shape),
            grad.reshape(volume.shape),
            fg.reshape(3, 3, 3, own, 32).transpose(3, 4, 0, 1, 2),
        )

    return jax.shard_map(
        shards,
        mesh=mesh,
        in_specs=(
            P("col", None, "gx", "gy"),
            P("col", None, None, None, None),
            P("col", None, "gx", "gy"),
        ),
        out_specs=(
            P("col", None, "gx", "gy"),
            P("col", None, "gx", "gy"),
            P("col", None, None, None, None),
        ),
        check_vma=False,
    )
```

profile of v0, /device:TPU:0, one launch (start us, length us, event | category | flops | bytes accessed | tf_op | source)
XLA Modules:
  0.0 27.7 jit_solution(12570781740205097442)
XLA Ops:
  0.6 0.0 copy-start
  0.6 0.9 %copy-done = f32[8,8,4,128]{3,2,1,0:T(4,128)S(1)} copy-done((f32[8,8,4,128]{3,2,1,0:T(4,128)S(1)}, f32[8,8,4,128]{3,2,1,0:T(4,128)}, u32[]{:S(2)}) %copy-start) | copy-done | bytes 131096
  1.5 0.0 copy-start.1
  1.5 0.9 %copy-done.1 = f32[8,8,4,128]{3,2,1,0:T(4,128)S(1)} copy-done((f32[8,8,4,128]{3,2,1,0:T(4,128)S(1)}, f32[8,8,4,128]{3,2,1,0:T(4,128)}, u32[]{:S(2)}) %copy-start.1) | copy-done | bytes 131096
  2.4 0.0 copy-start.2
  2.4 0.9 %copy-done.2 = f32[8,32,3,3,3]{1,0,4,3,2:T(8,128)S(1)} copy-done((f32[8,32,3,3,3]{1,0,4,3,2:T(8,128)S(1)}, f32[8,32,3,3,3]{1,0,4,3,2:T(8,128)}, u32[]{:S(2)}) %copy-start.2) | copy-done | bytes 27672
  3.3 22.4 %shard_map.58 = (f32[256,128]{1,0:T(8,128)S(1)}, f32[256,128]{1,0:T(8,128)S(1)}, f32[216,32]{1,0:T(8,128)S(1)}) custom-call(f32[256,128]{1,0:T(8,128)S(1)} %bitcast.10, f32[216,32]{1,0:T(8,128)S(1)} %bitcast.14, f32[256,128]{1,0:T(8,128)S(1)} %bitcast.11), custom_call_target="tpu_custom_call" | custom-call | tf_op jit(solution)/shard_map/pallas_call | solution.py:411
  25.8 0.7 %copy.9 = f32[8,8,4,128]{3,2,1,0:T(4,128)} copy(f32[8,8,4,128]{3,2,1,0:T(4,128)S(1)} %bitcast.13) | data formatting | bytes 262144
  26.4 0.7 %copy.10 = f32[8,8,4,128]{3,2,1,0:T(4,128)} copy(f32[8,8,4,128]{3,2,1,0:T(4,128)S(1)} %bitcast.12) | data formatting | bytes 262144
  27.1 0.6 %copy.11 = f32[8,32,3,3,3]{1,0,4,3,2:T(8,128)} copy(f32[8,32,3,3,3]{1,0,4,3,2:T(8,128)S(1)} %bitcast.15) | data formatting | bytes 55296
Async XLA Ops:
  0.6 0.9 %copy-start = (f32[8,8,4,128]{3,2,1,0:T(4,128)S(1)}, f32[8,8,4,128]{3,2,1,0:T(4,128)}, u32[]{:S(2)}) copy-start(f32[8,8,4,128]{3,2,1,0:T(4,128)} %param.3) | copy-start | bytes 393220
  1.5 0.9 %copy-start.1 = (f32[8,8,4,128]{3,2,1,0:T(4,128)S(1)}, f32[8,8,4,128]{3,2,1,0:T(4,128)}, u32[]{:S(2)}) copy-start(f32[8,8,4,128]{3,2,1,0:T(4,128)} %param.5) | copy-start | bytes 393220
  2.4 0.9 %copy-start.2 = (f32[8,32,3,3,3]{1,0,4,3,2:T(8,128)S(1)}, f32[8,32,3,3,3]{1,0,4,3,2:T(8,128)}, u32[]{:S(2)}) copy-start(f32[8,32,3,3,3]{1,0,4,3,2:T(8,128)} %param.4) | copy-start | bytes 82948
where the time goes:
time: 27.9 us; the launch traced here: 27.7 us
  Pallas kernels  22.4 us (80%)
  local copies, waits for them, and re-layouts  4.65 us (17%)
  between operations  0.65 us (2%)
    pallas_call x1, Pallas kernels, shards(): pl.pallas_call(functools.partial(kernel, nx, ny, planes, rows, scale), ou...  22.4 us
    unnamed x9, local copies, waits for them, and re-layouts  4.65 us

commit v1 on v0

--- a/solution.py
+++ b/solution.py
@@ -12,6 +12,7 @@
 BF16 = jnp.bfloat16
 DIRS = [(-1, 0), (1, 0), (-1, -1), (0, -1), (1, -1), (-1, 1), (0, 1), (1, 1)]
 TAPS = [(a, b, e) for a in range(3) for b in range(3) for e in range(3)]
+CHUNKS = 4
 PIECES = 7
 
 
@@ -33,6 +34,7 @@
     group = nx * ny
     me = gx * ny + gy
     cells = planes * rows
+    span = cells // CHUNKS
     low, high = col % 2, col // 2
     core = high * 2 + (1 - low)
     chip = (1 - high) * 2 + low
@@ -54,11 +56,6 @@
         load.start()
     barrier = pltpu.get_barrier_semaphore()
 
-    u_row[...] = jnp.zeros_like(u_row)
-    pack_in[...] = jnp.zeros_like(pack_in)
-    row_in[...] = jnp.zeros_like(row_in)
-    rpack_in[...] = jnp.zeros_like(rpack_in)
-
     for other in (core, chip):
         pl.semaphore_signal(barrier, inc=1, device_id={"col": other}, device_id_type=MESH)
 
@@ -71,6 +68,15 @@
         return carry
 
     lax.fori_loop(0, group, greet, 0)
+
+    for d, (dx, dy) in enumerate(DIRS):
+        @pl.when(jnp.logical_not(exists(-dx, -dy)))
+        def _():
+            for row, corner in ((u_row, pack_in), (row_in, rpack_in)):
+                if dy == 0:
+                    row[d] = jnp.zeros(row.shape[1:], F32)
+                else:
+                    corner[d - 2] = jnp.zeros((8, 128), F32)
 
     lane = lax.broadcasted_iota(jnp.int32, (8, 128), 1)
     loads[0].wait()
@@ -90,10 +96,11 @@
 
     pl.semaphore_wait(barrier, group + 1)
 
-    def v_copy(slot, sem, target):
-        return pltpu.make_async_remote_copy(
-            src_ref=vx.at[slot], dst_ref=vx.at[slot], send_sem=v_send.at[sem],
-            recv_sem=v_recv.at[sem], device_id={"col": target}, device_id_type=MESH,
+    def v_copy(slot, sem, target, k):
+        part = vx.at[slot, pl.ds(k * span, span)]
+        return pltpu.make_async_remote_copy(
+            src_ref=part, dst_ref=part, send_sem=v_send.at[sem, k],
+            recv_sem=v_recv.at[sem, k], device_id={"col": target}, device_id_type=MESH,
         )
 
     def u_copy(d):
@@ -126,9 +133,16 @@
                 getattr(copies(d), what)()
 
     each(u_copy, "start", True)
-    v_chip, v_core = v_copy(col, 0, chip), v_copy(col, 1, core)
-    v_chip.start()
-    v_core.start()
+    v_chip = [v_copy(col, 0, chip, k) for k in range(CHUNKS)]
+    v_core = [v_copy(col, 1, core, k) for k in range(CHUNKS)]
+    v_fwd = [v_copy(chip, 2, core, k) for k in range(CHUNKS)]
+    for k in range(CHUNKS):
+        v_chip[k].start()
+        v_core[k].start()
+
+    def hand_on(k):
+        v_chip[k].wait_recv()
+        v_fwd[k].start()
 
     loads[2].wait()
     w = w_in[...]
@@ -158,6 +172,7 @@
     w_back = jnp.concatenate(w_back, axis=0).astype(BF16)
 
     each(u_copy, "wait_recv", False)
+    hand_on(0)
     spot = lane % 8
     edge = jnp.zeros((8, 128), F32)
     for first, keep in ((3, lane < 64), (0, lane >= 64)):
@@ -209,7 +224,10 @@
                 )
         return carry
 
-    lax.fori_loop(0, planes, back, 0)
+    hand_on(1)
+    lax.fori_loop(0, planes // 2, back, 0)
+    hand_on(2)
+    lax.fori_loop(planes // 2, planes, back, 0)
 
     def g_copy(slot, to, target):
         return pltpu.make_async_remote_copy(
@@ -219,22 +237,12 @@
 
     g_far, g_core, g_chip = g_copy(far, 1, core), g_copy(core, 0, core), g_copy(chip, 2, chip)
     g_far.start()
-    v_chip.wait_recv()
-    v_fwd = v_copy(chip, 2, core)
-    v_fwd.start()
+    hand_on(3)
     g_core.start()
     g_far.wait_recv()
     for i in range(cells):
         igp[chip, i] = igp[chip, i] + rs[1, i]
     g_chip.start()
-
-    v_core.wait_recv()
-    for g in (col, chip, core):
-        for i in range(cells):
-            x2[g, i] = split(vx[g, i])
-    v_fwd.wait_recv()
-    for i in range(cells):
-        x2[far, i] = split(vx[far, i])
 
     def block(z):
         return jnp.concatenate(
@@ -248,7 +256,16 @@
     def weigh(z, total):
         return total + lax.dot_general(block(z), stack(z), nt, preferred_element_type=F32)
 
-    total = lax.fori_loop(0, planes, weigh, jnp.zeros((64, 2 * taps8), F32))
+    total = jnp.zeros((64, 2 * taps8), F32)
+    for k in range(CHUNKS):
+        v_core[k].wait_recv()
+        for g in (col, chip, core):
+            for i in range(k * span, (k + 1) * span):
+                x2[g, i] = split(vx[g, i])
+        v_fwd[k].wait_recv()
+        for i in range(k * span, (k + 1) * span):
+            x2[far, i] = split(vx[far, i])
+        total = lax.fori_loop(k * planes // CHUNKS, (k + 1) * planes // CHUNKS, weigh, total)
     folded = jnp.concatenate(
         [total[g * 16 : g * 16 + 8] + total[g * 16 + 8 : g * 16 + 16] for g in range(4)], axis=0
     )
@@ -381,7 +398,7 @@
 
     each(u_copy, "wait_send", True)
     each(r_copy, "wait_send", True)
-    for copy in (v_chip, v_core, v_fwd, g_far, g_core, g_chip):
+    for copy in (*v_chip, *v_core, *v_fwd, g_far, g_core, g_chip):
         copy.wait_send()
     for i in range(PIECES):
         @pl.when(me != i)
@@ -439,8 +456,8 @@
                 pltpu.VMEM((nx * ny,) + tile, F32),
                 pltpu.VMEM((PIECES,) + tile, F32),
                 pltpu.SemaphoreType.DMA((3,)),
-                pltpu.SemaphoreType.DMA((3,)),
-                pltpu.SemaphoreType.DMA((3,)),
+                pltpu.SemaphoreType.DMA((3, CHUNKS)),
+                pltpu.SemaphoreType.DMA((3, CHUNKS)),
                 pltpu.SemaphoreType.DMA((8,)),
                 pltpu.SemaphoreType.DMA((8,)),
                 pltpu.SemaphoreType.DMA((3,)),
@@ -453,7 +470,7 @@
                 pltpu.SemaphoreType.DMA((PIECES,)),
             ],
             compiler_params=pltpu.CompilerParams(
-                collective_id=0, has_side_effects=True, vmem_limit_bytes=40 * 1024 * 1024
+                collective_id=0, has_side_effects=True, vmem_limit_bytes=63 * 1024 * 1024
             ),
         )(
             volume.reshape(own * cells, width),

time: 27.9 us -> 27.2 us (0.975)
  local copies, waits for them, and re-layouts: 4.65 us -> 3.19 us
  Pallas kernels: 22.4 us -> 23.2 us
    unnamed x9 -> x7, local copies, waits for them, and re-layouts: 4.65 us -> 3.19 us
    pallas_call x1, Pallas kernels: 22.4 us -> 23.2 us  [shards(): pl.pallas_call(functools.partial(kernel, nx, ny, planes, rows, scale), ou...]
where the time goes in v1:
time: 27.2 us; the launch traced here: 27.1 us
  Pallas kernels  23.2 us (85%)
  local copies, waits for them, and re-layouts  3.19 us (12%)
  between operations  0.65 us (2%)
    pallas_call x1, Pallas kernels, shards(): pl.pallas_call(functools.partial(kernel, nx, ny, planes, rows, scale), ou...  23.2 us
    unnamed x7, local copies, waits for them, and re-layouts  3.19 us

profile of v1, /device:TPU:0, one launch (start us, length us, event | category | flops | bytes accessed | tf_op | source)
XLA Modules:
  0.0 27.1 jit_solution(7303733070744677807)
XLA Ops:
  0.6 23.2 %shard_map.58 = (f32[256,128]{1,0:T(8,128)}, f32[256,128]{1,0:T(8,128)}, f32[216,32]{1,0:T(8,128)}) custom-call(f32[256,128]{1,0:T(8,128)} %bitcast.10, f32[216,32]{1,0:T(8,128)} %bitcast.14, f32[256,128]{1,0:T(8,128)} %bitcast.11), custom_call_target="tpu_custom_call" | custom-call | tf_op jit(solution)/shard_map/pallas_call | solution.py:428
  23.9 0.0 copy-start
  23.9 1.6 %copy.9 = f32[8,8,4,128]{3,2,1,0:T(4,128)} copy(f32[8,8,4,128]{3,2,1,0:T(4,128)} %bitcast.13) | data formatting | bytes 262144
  25.5 0.0 copy-done
  25.5 0.0 copy-start.1
  25.5 0.7 %copy.10 = f32[8,8,4,128]{3,2,1,0:T(4,128)} copy(f32[8,8,4,128]{3,2,1,0:T(4,128)S(1)} %bitcast.12) | data formatting | bytes 262144
  26.1 0.3 %copy-done.1 = f32[216,32]{1,0:T(8,128)S(1)} copy-done((f32[216,32]{1,0:T(8,128)S(1)}, f32[216,32]{1,0:T(8,128)}, u32[]{:S(2)}) %copy-start.1) | copy-done | bytes 27672
  26.4 0.6 %copy.11 = f32[8,32,3,3,3]{1,0,4,3,2:T(8,128)} copy(f32[8,32,3,3,3]{1,0,4,3,2:T(8,128)S(1)} %bitcast.15) | data formatting | bytes 55296
Async XLA Ops:
  23.9 1.6 %copy-start = (f32[256,128]{1,0:T(8,128)S(1)}, f32[256,128]{1,0:T(8,128)}, u32[]{:S(2)}) copy-start(f32[256,128]{1,0:T(8,128)} %get-tuple-element.7) | copy-start | bytes 393220
  25.5 0.9 %copy-start.1 = (f32[216,32]{1,0:T(8,128)S(1)}, f32[216,32]{1,0:T(8,128)}, u32[]{:S(2)}) copy-start(f32[216,32]{1,0:T(8,128)} %get-tuple-element.8) | copy-start | bytes 82948

commit v2 on v1

--- a/solution.py
+++ b/solution.py
@@ -256,6 +256,25 @@
     def weigh(z, total):
         return total + lax.dot_general(block(z), stack(z), nt, preferred_element_type=F32)
 
+    acc[...] = jnp.zeros_like(acc)
+
+    def forward(z, carry):
+        cell = block(z)
+        y = jnp.dot(w_fwd, jnp.concatenate([cell, cell], axis=0), preferred_element_type=F32)
+        for a in range(3):
+            for e in range(3):
+                for x in range(rows + 2):
+                    terms = [
+                        y[
+                            ((a * 3 + b) * 3 + e) * 8 : ((a * 3 + b) * 3 + e) * 8 + 8,
+                            (x + b - 2) * 128 : (x + b - 1) * 128,
+                        ]
+                        for b in range(3)
+                        if 0 <= x + b - 2 < rows
+                    ]
+                    acc[e, z + 2 - a, x] = functools.reduce(lambda s, t: s + t, terms, acc[e, z + 2 - a, x])
+        return carry
+
     total = jnp.zeros((64, 2 * taps8), F32)
     for k in range(CHUNKS):
         v_core[k].wait_recv()
@@ -266,6 +285,8 @@
         for i in range(k * span, (k + 1) * span):
             x2[far, i] = split(vx[far, i])
         total = lax.fori_loop(k * planes // CHUNKS, (k + 1) * planes // CHUNKS, weigh, total)
+        if k < CHUNKS - 1:
+            lax.fori_loop(k * planes // CHUNKS, (k + 1) * planes // CHUNKS, forward, 0)
     folded = jnp.concatenate(
         [total[g * 16 : g * 16 + 8] + total[g * 16 + 8 : g * 16 + 16] for g in range(4)], axis=0
     )
@@ -294,26 +315,7 @@
         def _():
             s1_copy(i).start()
 
-    acc[...] = jnp.zeros_like(acc)
-
-    def forward(z, carry):
-        cell = block(z)
-        y = jnp.dot(w_fwd, jnp.concatenate([cell, cell], axis=0), preferred_element_type=F32)
-        for a in range(3):
-            for e in range(3):
-                for x in range(rows + 2):
-                    terms = [
-                        y[
-                            ((a * 3 + b) * 3 + e) * 8 : ((a * 3 + b) * 3 + e) * 8 + 8,
-                            (x + b - 2) * 128 : (x + b - 1) * 128,
-                        ]
-                        for b in range(3)
-                        if 0 <= x + b - 2 < rows
-                    ]
-                    acc[e, z + 2 - a, x] = functools.reduce(lambda s, t: s + t, terms, acc[e, z + 2 - a, x])
-        return carry
-
-    lax.fori_loop(0, planes, forward, 0)
+    lax.fori_loop(planes - planes // CHUNKS, planes, forward, 0)
     pack = jnp.zeros((8, 128), F32)
     for z in range(planes):
         for x in range(rows + 2):

time: 27.2 us -> 28.6 us (1.051)
  Pallas kernels: 23.2 us -> 24.6 us
    pallas_call x1, Pallas kernels: 23.2 us -> 24.6 us  [shards(): pl.pallas_call(functools.partial(kernel, nx, ny, planes, rows, scale), ou...]
where the time goes in v2:
time: 28.6 us; the launch traced here: 28.4 us
  Pallas kernels  24.6 us (86%)
  local copies, waits for them, and re-layouts  3.19 us (11%)
  between operations  0.65 us (2%)
    pallas_call x1, Pallas kernels, shards(): pl.pallas_call(functools.partial(kernel, nx, ny, planes, rows, scale), ou...  24.6 us
    unnamed x7, local copies, waits for them, and re-layouts  3.19 us

profile of v2, /device:TPU:0, one launch (start us, length us, event | category | flops | bytes accessed | tf_op | source)
XLA Modules:
  0.0 28.4 jit_solution(3507455156463528962)
XLA Ops:
  0.6 24.6 %shard_map.58 = (f32[256,128]{1,0:T(8,128)}, f32[256,128]{1,0:T(8,128)}, f32[216,32]{1,0:T(8,128)}) custom-call(f32[256,128]{1,0:T(8,128)} %bitcast.10, f32[216,32]{1,0:T(8,128)} %bitcast.14, f32[256,128]{1,0:T(8,128)} %bitcast.11), custom_call_target="tpu_custom_call" | custom-call | tf_op jit(solution)/shard_map/pallas_call | solution.py:430
  25.2 0.0 copy-start
  25.2 1.6 %copy.9 = f32[8,8,4,128]{3,2,1,0:T(4,128)} copy(f32[8,8,4,128]{3,2,1,0:T(4,128)} %bitcast.13) | data formatting | bytes 262144
  26.8 0.0 copy-done
  26.8 0.0 copy-start.1
  26.8 0.7 %copy.10 = f32[8,8,4,128]{3,2,1,0:T(4,128)} copy(f32[8,8,4,128]{3,2,1,0:T(4,128)S(1)} %bitcast.12) | data formatting | bytes 262144
  27.5 0.3 %copy-done.1 = f32[216,32]{1,0:T(8,128)S(1)} copy-done((f32[216,32]{1,0:T(8,128)S(1)}, f32[216,32]{1,0:T(8,128)}, u32[]{:S(2)}) %copy-start.1) | copy-done | bytes 27672
  27.8 0.6 %copy.11 = f32[8,32,3,3,3]{1,0,4,3,2:T(8,128)} copy(f32[8,32,3,3,3]{1,0,4,3,2:T(8,128)S(1)} %bitcast.15) | data formatting | bytes 55296
Async XLA Ops:
  25.2 1.6 %copy-start = (f32[256,128]{1,0:T(8,128)S(1)}, f32[256,128]{1,0:T(8,128)}, u32[]{:S(2)}) copy-start(f32[256,128]{1,0:T(8,128)} %get-tuple-element.7) | copy-start | bytes 393220
  26.8 0.9 %copy-start.1 = (f32[216,32]{1,0:T(8,128)S(1)}, f32[216,32]{1,0:T(8,128)}, u32[]{:S(2)}) copy-start(f32[216,32]{1,0:T(8,128)} %get-tuple-element.8) | copy-start | bytes 82948
